TPU v7x, 128 devices: a whole 4x4x4 slice. The times are simulated.
128 devices in a mesh: pass: 16 (over x, y), query: 8 (over z, core).
Axes of the slice: x: 4, y: 4, z: 4, core: 2. Of those that a mesh axis runs over, the one named last changes fastest.
Arguments:
- query_q: bfloat16 [16384, 4096], P(('pass', 'query')), may hold values from -6 to 6
- query_k: bfloat16 [16384, 512], P(('pass', 'query')), may hold values from -6 to 6
- query_v: bfloat16 [16384, 512], P(('pass', 'query')), may hold values from -0.5 to 0.5
- query_out: bfloat16 [16384, 4096], P(('pass', 'query')), may hold values from -0.5 to 0.5
- query_dout: bfloat16 [16384, 4096], P(('pass', 'query')), may hold values from -6 to 6
- query_lse: float32 [32, 16384], P(None, ('pass', 'query')), may hold values from 7 to 9
- query_seg: int32 [16, 1024], P('pass'), may hold values from 0 to 3, never falling along the last dimension, each value on 1 to 512 neighbouring positions
- passage_q: bfloat16 [8192, 4096], P(('pass', 'query')), may hold values from -6 to 6
- passage_k: bfloat16 [8192, 512], P(('pass', 'query')), may hold values from -6 to 6
- passage_v: bfloat16 [8192, 512], P(('pass', 'query')), may hold values from -0.5 to 0.5
- passage_out: bfloat16 [8192, 4096], P(('pass', 'query')), may hold values from -0.5 to 0.5
- passage_dout: bfloat16 [8192, 4096], P(('pass', 'query')), may hold values from -6 to 6
- passage_lse: float32 [32, 8192], P(None, ('pass', 'query')), may hold values from 4.5 to 6.5
- passage_len: int32 [16], replicated, may hold values from 384 to 512, as said below
- reads: int32 [16, 8], replicated, may hold values from 0 to 15, as said below
Outputs:
- query_dq: bfloat16 [16384, 4096], P(('pass', 'query'))
- query_dk: bfloat16 [16384, 512], P(('pass', 'query'))
- query_dv: bfloat16 [16384, 512], P(('pass', 'query'))
- passage_dq: bfloat16 [8192, 4096], P(('pass', 'query'))
- passage_dk: bfloat16 [8192, 512], P(('pass', 'query'))
- passage_dv: bfloat16 [8192, 512], P(('pass', 'query'))
Inputs may be any that keep to these rules, and one draw needn't show every extreme that they name: `passage_len`: some passage has exactly 512 live tokens and some exactly 384. `reads`: each row lists 8 different passages; every passage is listed by some block. `query_seg`: within each query block the document ids never fall; each document has 1 to 512 positions, one exactly 512.
All inputs are finite; a program needn't handle non-finite values.
Results may differ from a plain program's by a relative error of at most 0.018.
Values may be sent and summed in bfloat16 or wider, within the bound.
A program may use at most 192 MiB of HBM per device.

v0:
```python
import math

import jax
import jax.numpy as jnp
from jax import lax
from jax.sharding import PartitionSpec as P

H = 32
KVH = 4
HD = 128


def attend_back(queries, keys, values, out_grad, log_norm, deltas, visible):
    query_rows = queries.shape[0]
    key_rows = keys.shape[0]
    groups = H // KVH
    scaling = HD ** (-0.5)
    query_heads = queries.reshape(query_rows, KVH, groups, HD)
    grad_heads = out_grad.reshape(query_rows, KVH, groups, HD)
    key_heads = keys.reshape(key_rows, KVH, HD)
    value_heads = values.reshape(key_rows, KVH, HD)
    norm_heads = log_norm.reshape(KVH, groups, query_rows)
    delta_heads = deltas.reshape(KVH, groups, query_rows)
    scores = (
        jnp.einsum("qkgd,tkd->kgqt", query_heads, key_heads, preferred_element_type=jnp.float32)
        * scaling
    )
    weights = jnp.where(visible, jnp.exp(scores - norm_heads[..., None]), 0.0)
    weight_grad = jnp.einsum(
        "qkgd,tkd->kgqt", grad_heads, value_heads, preferred_element_type=jnp.float32
    )
    score_grad = weights * (weight_grad - delta_heads[..., None])
    weights_low = weights.astype(jnp.bfloat16)
    score_low = score_grad.astype(jnp.bfloat16)
    value_grad = jnp.einsum(
        "kgqt,qkgd->tkd", weights_low, grad_heads, preferred_element_type=jnp.float32
    ).reshape(key_rows, KVH * HD)
    key_grad = (
        jnp.einsum(
            "kgqt,qkgd->tkd", score_low, query_heads, preferred_element_type=jnp.float32
        ).reshape(key_rows, KVH * HD)
        * scaling
    )
    query_grad = (
        jnp.einsum(
            "kgqt,tkd->qkgd", score_low, key_heads, preferred_element_type=jnp.float32
        ).reshape(query_rows, H * HD)
        * scaling
    )
    return (query_grad, key_grad, value_grad)


def row_delta(out_grad, outputs):
    product = out_grad.astype(jnp.float32) * outputs.astype(jnp.float32)
    return jnp.sum(product.reshape(-1, H, HD), axis=2).T


def shards(
    query_q,
    query_k,
    query_v,
    query_out,
    query_dout,
    query_lse,
    query_seg,
    passage_q,
    passage_k,
    passage_v,
    passage_out,
    passage_dout,
    passage_lse,
    passage_len,
    reads,
):
    kv_width = KVH * HD
    pair_width = 2 * kv_width
    query_tokens = query_q.shape[0]
    passage_rows = passage_q.shape[0]
    pass_count = lax.axis_size("pass")
    query_count = lax.axis_size("query")
    passage_span = passage_rows * query_count
    read_count = reads.shape[1]
    own_block = lax.axis_index("pass")
    own_row = lax.axis_index("query")
    query_delta = row_delta(query_dout, query_out)
    passage_delta = row_delta(passage_dout, passage_out)
    positions = jnp.arange(passage_span, dtype=jnp.int32)
    live = positions[None, :] < passage_len[:, None]
    own_reads = lax.dynamic_index_in_dim(reads, own_block, 0, keepdims=False)
    read_live = jnp.take(live, own_reads, axis=0)
    reading = jnp.any(
        reads[:, :, None] == jnp.arange(pass_count, dtype=jnp.int32)[None, None, :], axis=1
    )
    wanted = lax.dynamic_index_in_dim(reading, own_block, 1, keepdims=False)
    self_pairs = jnp.concatenate([query_k, query_v], axis=1)
    own_pairs = jnp.concatenate([passage_k, passage_v], axis=1)
    outgoing = jnp.where(wanted[:, None, None], own_pairs[None], jnp.zeros((), jnp.bfloat16))
    spread = jnp.broadcast_to(
        outgoing[:, None], (pass_count, query_count, passage_rows, pair_width)
    )
    incoming = lax.all_to_all(
        spread.reshape(-1, pair_width), ("pass", "query"), split_axis=0, concat_axis=0, tiled=True
    )
    read_pairs = jnp.take(incoming.reshape(pass_count, passage_span, pair_width), own_reads, axis=0)
    shard = jnp.concatenate([self_pairs, own_pairs], axis=0)
    shard_rows = shard.shape[0]
    segments = query_seg[0]
    own_pos = own_row * query_tokens + jnp.arange(query_tokens, dtype=jnp.int32)
    own_segments = lax.dynamic_slice_in_dim(segments, own_row * query_tokens, query_tokens, 0)
    local_pos = own_row * passage_rows + jnp.arange(passage_rows, dtype=jnp.int32)
    own_length = lax.dynamic_index_in_dim(passage_len, own_block, 0, keepdims=False)
    local_live = local_pos < own_length
    piece = lax.all_gather(shard, "query", axis=0, tiled=True)
    count = piece.shape[0] // shard_rows
    parts = piece.reshape(count, shard_rows, pair_width)
    self_keys = parts[:, :query_tokens].reshape(count * query_tokens, pair_width)
    key_pos = jnp.arange(count * query_tokens, dtype=jnp.int32)
    self_visible = (key_pos[None, :] <= own_pos[:, None]) & (
        segments[None, :] == own_segments[:, None]
    )
    query_grad, self_k, self_v = attend_back(
        query_q,
        self_keys[:, :kv_width],
        self_keys[:, kv_width:],
        query_dout,
        query_lse,
        query_delta,
        self_visible,
    )
    local_keys = parts[:, query_tokens : query_tokens + passage_rows].reshape(
        count * passage_rows, pair_width
    )
    local_key_pos = jnp.arange(count * passage_rows, dtype=jnp.int32)
    local_visible = (
        (local_key_pos[None, :] <= local_pos[:, None])
        & (local_key_pos[None, :] < own_length)
        & local_live[:, None]
    )
    local_grad, local_k, local_v = attend_back(
        passage_q,
        local_keys[:, :kv_width],
        local_keys[:, kv_width:],
        passage_dout,
        passage_lse,
        passage_delta,
        local_visible,
    )
    pieces = [
        jnp.concatenate([self_k, self_v], axis=1).reshape(count, query_tokens, pair_width),
        jnp.concatenate([local_k, local_v], axis=1).reshape(count, passage_rows, pair_width),
    ]
    piece_grads = jnp.concatenate(pieces, axis=1).reshape(count * shard_rows, pair_width)
    query_total = query_grad
    summed = lax.psum_scatter(
        piece_grads.astype(jnp.bfloat16), "query", scatter_dimension=0, tiled=True
    ).astype(jnp.float32)
    key_count = read_count * passage_span
    key_block = math.gcd(key_count, 512)

    def visit_block(grad_total, inputs):
        pair_block, live_block = inputs
        visible = jnp.broadcast_to(live_block[None, :], (query_tokens, key_block))
        grad_part, key_part, value_part = attend_back(
            query_q,
            pair_block[:, :kv_width],
            pair_block[:, kv_width:],
            query_dout,
            query_lse,
            query_delta,
            visible,
        )
        return (grad_total + grad_part, jnp.concatenate([key_part, value_part], axis=1))

    read_query_grad, read_grads = lax.scan(
        visit_block, jnp.zeros((query_tokens, H * HD), jnp.float32), (read_pairs, read_live)
    )
    query_total = query_total + read_query_grad
    read_low = read_grads.astype(jnp.bfloat16)
    expanded = (
        jnp.zeros((pass_count, passage_span, pair_width), jnp.bfloat16).at[own_reads].set(read_low)
    )
    returned_rows = lax.all_to_all(
        expanded.reshape(-1, pair_width), ("pass", "query"), split_axis=0, concat_axis=0, tiled=True
    )
    reader_sum = jnp.sum(
        returned_rows.astype(jnp.float32).reshape(
            pass_count * query_count, passage_rows, pair_width
        ),
        axis=0,
    )
    passage_sum = summed[query_tokens : query_tokens + passage_rows] + reader_sum
    query_dq = query_total.astype(jnp.bfloat16)
    query_dk = summed[:query_tokens, :kv_width].astype(jnp.bfloat16)
    query_dv = summed[:query_tokens, kv_width:].astype(jnp.bfloat16)
    passage_dq = local_grad.astype(jnp.bfloat16)
    passage_dk = passage_sum[:, :kv_width].astype(jnp.bfloat16)
    passage_dv = passage_sum[:, kv_width:].astype(jnp.bfloat16)
    return (query_dq, query_dk, query_dv, passage_dq, passage_dk, passage_dv)


def solution(mesh):
    placed = (
        P(("pass", "query"), None),
        P(("pass", "query"), None),
        P(("pass", "query"), None),
        P(("pass", "query"), None),
        P(("pass", "query"), None),
        P(None, ("pass", "query")),
        P("pass", None),
        P(("pass", "query"), None),
        P(("pass", "query"), None),
        P(("pass", "query"), None),
        P(("pass", "query"), None),
        P(("pass", "query"), None),
        P(None, ("pass", "query")),
        P(),
        P(),
    )
    return jax.shard_map(
        shards,
        mesh=mesh,
        in_specs=placed,
        out_specs=(
            P(("pass", "query"), None),
            P(("pass", "query"), None),
            P(("pass", "query"), None),
            P(("pass", "query"), None),
            P(("pass", "query"), None),
            P(("pass", "query"), None),
        ),
        check_vma=False,
    )
```

profile of v0, /device:TPU:50, one launch (start us, length us, event | category | flops | bytes accessed | tf_op | source)
XLA Modules:
  0.0 695.0 jit_solution(4267759891926189745)
XLA Ops:
  10.1 6.1 broadcast_in_dim.114
  16.2 10.6 %all-to-all-start = ((bf16[128,64,1024]{2,1,0:T(8,128)(2,1)}), bf16[128,64,1024]{2,1,0:T(8,128)(2,1)}, u32[]{:S(2)}, u32[]{:S(2)}) async-start(bf16[128,64,1024]{2,1,0:T(8,128)(2,1)} %bitcast.298), calls=%async_computation | async-start | bytes 33554432 | tf_op jit(solution)/shard_map/all_to_all | solution.py:101
  28.6 1.3 copy.261
  29.9 1.5 multiply_bitcast_fusion
  33.2 221.7 %all-to-all-done = bf16[128,64,1024]{2,1,0:T(8,128)(2,1)} async-done(((bf16[128,64,1024]{2,1,0:T(8,128)(2,1)}), bf16[128,64,1024]{2,1,0:T(8,128)(2,1)}, u32[]{:S(2)}, u32[]{:S(2)}) %all-to-all-start) | async-done | bytes 16777248 | tf_op jit(solution)/shard_map/all_to_all | solution.py:101
  254.9 10.5 %gather_fusion = bf16[8,512,1024]{2,1,0:T(8,128)(2,1)} fusion(bf16[16,512,1024]{2,1,0:T(8,128)(2,1)} %bitcast.18, s32[1024]{0:T(1024)S(1)} %pad_clamp_fusion), kind=kCustom, calls=%fused_computation | custom fusion | bytes 16777248 | tf_op jit(solution)/shard_map/jit(_take)/gather | solution.py:104
  265.4 7.6 %broadcast_select_fusion = bf16[8,512,1024]{2,1,0:T(8,128)(2,1)} fusion(bf16[8,512,1024]{2,1,0:T(8,128)(2,1)} %gather_fusion, pred[8]{0:T(512)(128)(4,1)S(1)} %compare_and_fusion), kind=kLoop, calls=%fused_computation.31 | loop fusion | flops 4194304 | bytes 16777224 | tf_op jit(solution)/shard_map/jit(_take)/select_n | solution.py:104
  273.0 109.8 %while.13 = (s32[]{:T(128)}, f32[128,4096]{0,1:T(8,128)}, bf16[8,512,1024]{1,2,0:T(8,128)(2,1)}, bf16[8,512,1024]{2,1,0:T(8,128)(2,1)}, pred[8,512]{1,0:T(8,128)...) while((s32[]{:T(128)}, f32[128,4096]{0,1:T(8,128)}, ...), condition=%wide.region_3.4_spmd.clone, body=%wide.region_2.3_spmd.clone.sunk | while | flops 2709520384 | bytes 82364648 | solution.py:174
  273.0 1.3 constant_dynamic-slice_fusion.3
  276.3 2.1 fusion.126
  278.4 3.1 fusion.125
  281.5 1.5 fusion.127
  290.0 2.1 fusion.126
  292.1 3.1 fusion.125
  295.3 1.5 fusion.127
  303.7 2.1 fusion.126
  305.8 3.1 fusion.125
  309.0 1.5 fusion.127
  317.4 2.1 fusion.126
  319.6 3.1 fusion.125
  322.7 1.5 fusion.127
  331.2 2.1 fusion.126
  333.3 3.1 fusion.125
  336.5 1.5 fusion.127
  344.9 2.1 fusion.126
  347.0 3.1 fusion.125
  350.2 1.5 fusion.127
  358.6 2.1 fusion.126
  360.7 3.1 fusion.125
  363.9 1.5 fusion.127
  372.3 2.1 fusion.126
  374.5 3.1 fusion.125
  377.6 1.5 fusion.127
  382.8 11.5 %copy.285 = bf16[8,512,1024]{2,1,0:T(8,128)(2,1)} copy(bf16[8,512,1024]{1,2,0:T(8,128)(2,1)} %get-tuple-element.282) | data formatting | bytes 16777216 | tf_op jit(solution)/shard_map/convert_element_type | solution.py:178
  394.3 6.0 broadcast_in_dim.120
  400.3 21.3 %scatter_fusion = bf16[16,512,1024]{2,1,0:T(8,128)(2,1)} fusion(bf16[16,512,1024]{2,1,0:T(8,128)(2,1)} %broadcast_in_dim.120, s32[8]{0:T(128)S(1)} %fusion.67, bf16[8,512,1024]{2,1,0:T(8,128)(2,1)} %copy.285), kind=kCustom, calls=%fused_computation.2 | custom fusion | bytes 25165856 | tf_op jit(solution)/shard_map/scatter | solution.py:180
  421.6 16.7 %all-to-all-start.1 = ((bf16[128,64,1024]{2,1,0:T(8,128)(2,1)}), bf16[128,64,1024]{2,1,0:T(8,128)(2,1)}, u32[]{:S(2)}, u32[]{:S(2)}) async-start(bf16[128,64,1024]{2,1,0:T(8,128)(2,1)} %bitcast.294), calls=%async_computation.2 | async-start | bytes 33554432 | tf_op jit(solution)/shard_map/all_to_all | solution.py:182
  447.6 1.3 slice.69
  448.9 1.9 slice.66
  453.8 1.3 copy.328
  455.2 1.3 copy.269
  456.5 1.7 copy.327
  459.0 1.6 fusion.21
  460.9 1.4 copy-done.13
  463.4 3.7 fusion.49
  467.3 1.5 reshape.242
  468.8 1.5 reshape.241
  470.3 3.6 fusion.55
  474.0 11.0 %fusion.13 = bf16[4,8,128,1024]{2,3,1,0:T(8,128)(2,1)} fusion(f32[4,1024,128,8]{2,1,3,0:T(8,128)S(1)} %fusion.55, bf16[1024,4,128,1]{0,2,3,1:T(8,128)(2,1)} %bitcast.330, f32[4,8,128]{2,1,0:T(8,128)} %bitcast.339, f32[4,8,128]{2,1,0:T(8,128)} %bitcast.346, pred[128,1024]{0,1:T(8,128)(4,1)} %fusion.57, bf16[128,4,8,128]{3,2,1,0:T(8,128)(2,1)} %bitcast.328), kind=kOutput, calls=%fused_computation.25 | convolution fusion | flops 1098907648 | bytes 27426816 | tf_op jit(solution)/shard_map/qkgd,tkd->kgqt/dot_general | solution.py:29
  485.0 7.0 %fusion.35 = bf16[1024,4,128]{2,0,1:T(8,128)(2,1)} fusion(bf16[4,8,128,1024]{2,3,1,0:T(8,128)(2,1)} %fusion.13, bf16[128,4,8,128]{3,2,1,0:T(8,128)(2,1)} %bitcast.312), kind=kOutput, calls=%fused_computation.55 | convolution fusion | flops 1074790400 | bytes 10485760 | tf_op jit(solution)/shard_map/kgqt,qkgd->tkd/dot_general | solution.py:39
  492.0 1.6 copy.266
  494.8 9.9 %fusion.36 = bf16[1024,4,128]{2,0,1:T(8,128)(2,1)} fusion(f32[4,1024,128,8]{2,1,3,0:T(8,128)} %copy-done.3, f32[4,8,128]{2,1,0:T(8,128)S(1)} %bitcast.347, pred[128,1024]{0,1:T(8,128)(4,1)S(1)} %copy-done.22, bf16[128,4,8,128]{3,2,1,0:T(8,128)(2,1)S(1)} %bitcast.329), kind=kOutput, calls=%fused_computation.56 | convolution fusion | flops 1091043328 | bytes 19021824 | tf_op jit(solution)/shard_map/kgqt,qkgd->tkd/dot_general | solution.py:35
  504.7 1.6 copy.268
  506.6 11.5 %maximum_maximum_fusion = bf16[8,192,1024]{1,0,2:T(8,128)(2,1)} fusion(bf16[8,64,512]{1,0,2:T(8,128)(2,1)S(1)} %copy-done.11, bf16[8,64,512]{1,0,2:T(8,128)(2,1)} %reshape.241, bf16[8,128,512]{1,0,2:T(8,128)(2,1)S(1)} %bitcast.319, bf16[8,128,512]{1,0,2:T(8,128)(2,1)} %bitcast.318), kind=kLoop, calls=%fused_computation.33 | loop fusion | flops 12582912 | bytes 6291456 | tf_op jit(solution)/shard_map/concatenate | solution.py:152
  518.1 6.8 copy.282
  524.9 2.3 fusion.48
  528.6 6.0 convolution_multiply_fusion.1
  534.6 3.1 copy.263
  537.7 96.1 %reduce-scatter.2.cloned.1.call-done = bf16[192,1024]{1,0:T(8,128)(2,1)} async-done(((bf16[1536,1024]{1,0:T(8,128)(2,1)}), bf16[192,1024]{1,0:T(8,128)(2,1)}) %reduce-scatter.2.cloned.1.call-update) | async-done | bytes 393232 | tf_op jit(solution)/shard_map/reduce_scatter | solution.py:154
  633.8 1.7 fusion.75
  635.5 1.8 copy.264
  637.4 3.4 add_convert_fusion
  640.8 38.4 %all-to-all-done.1 = bf16[128,64,1024]{2,1,0:T(8,128)(2,1)} async-done(((bf16[128,64,1024]{2,1,0:T(8,128)(2,1)}), bf16[128,64,1024]{2,1,0:T(8,128)(2,1)}, u32[]{:S(2)}, u32[]{:S(2)}) %all-to-all-start.1) | async-done | bytes 16777248 | tf_op jit(solution)/shard_map/all_to_all | solution.py:182
  679.2 6.9 convert_reduce_fusion
  (226 shorter events, 79.3 us)
Async XLA Ops:
  16.2 10.7 %copy-start.23 = (bf16[128,512]{1,0:T(8,128)(2,1)S(1)}, bf16[128,512]{1,0:T(8,128)(2,1)}, u32[]{:S(2)}) copy-start(bf16[128,512]{1,0:T(8,128)(2,1)} %param.19) | copy-start | bytes 393220
  16.2 10.7 %copy-start.24 = (bf16[128,512]{1,0:T(8,128)(2,1)S(1)}, bf16[128,512]{1,0:T(8,128)(2,1)}, u32[]{:S(2)}) copy-start(bf16[128,512]{1,0:T(8,128)(2,1)} %param.18) | copy-start | bytes 393220
  16.2 11.5 %copy-start.28 = (s32[16,8]{0,1:T(8,128)S(1)}, s32[16,8]{0,1:T(8,128)}, u32[]{:S(2)}) copy-start(s32[16,8]{0,1:T(8,128)} %param.31) | copy-start | bytes 1540
  16.2 11.7 %copy-start.9 = (bf16[128,4096]{1,0:T(8,128)(2,1)S(1)}, bf16[128,4096]{1,0:T(8,128)(2,1)}, u32[]{:S(2)}) copy-start(bf16[128,4096]{1,0:T(8,128)(2,1)} %param.17) | copy-start | bytes 3145732
  16.2 12.4 %copy-start.4 = (bf16[128,4096]{1,0:T(8,128)(2,1)S(1)}, bf16[128,4096]{1,0:T(8,128)(2,1)}, u32[]{:S(2)}) copy-start(bf16[128,4096]{1,0:T(8,128)(2,1)} %param.21) | copy-start | bytes 3145732
  16.2 238.7 %all-to-all-start = ((bf16[128,64,1024]{2,1,0:T(8,128)(2,1)}), bf16[128,64,1024]{2,1,0:T(8,128)(2,1)}, u32[]{:S(2)}, u32[]{:S(2)}) async-start(bf16[128,64,1024]{2,1,0:T(8,128)(2,1)} %bitcast.298), calls=%async_computation | async-start | bytes 33554432 | tf_op jit(solution)/shard_map/all_to_all | solution.py:101
  26.8 420.8 %all-gather.2.cloned.1.call-start = ((), (), s32[]{:S(2)}) async-start(), calls=%async_computation.3 | async-start | bytes 3538944 | tf_op jit(solution)/shard_map/all_gather | solution.py:113
  31.4 1.1 copy-start.30
  265.4 7.6 %copy-start.15 = (bf16[128,4096]{0,1:T(8,128)(2,1)S(1)}, bf16[128,4096]{0,1:T(8,128)(2,1)}, u32[]{:S(2)}) copy-start(bf16[128,4096]{0,1:T(8,128)(2,1)} %copy.261) | copy-start | bytes 3145732
  265.4 7.6 %copy-start.32 = (f32[32,128]{1,0:T(8,128)S(1)}, f32[32,128]{1,0:T(8,128)}, u32[]{:S(2)}) copy-start(f32[32,128]{1,0:T(8,128)} %param.22) | copy-start | bytes 49156
  274.9 1.3 copy-start.16
  283.0 1.6 copy-start
  285.0 1.7 copy-start.1
  288.7 1.3 copy-start.16
  296.8 1.6 copy-start
  298.8 1.7 copy-start.1
  302.4 1.3 copy-start.16
  310.5 1.6 copy-start
  312.5 1.7 copy-start.1
  316.1 1.3 copy-start.16
  324.2 1.6 copy-start
  326.2 1.7 copy-start.1
  329.9 1.3 copy-start.16
  338.0 1.6 copy-start
  340.0 1.7 copy-start.1
  343.6 1.3 copy-start.16
  351.7 1.6 copy-start
  353.7 1.6 copy-start.1
  357.3 1.3 copy-start.16
  365.4 1.6 copy-start
  367.4 1.7 copy-start.1
  371.0 1.3 copy-start.16
  379.1 1.6 copy-start
  381.1 1.6 copy-start.1
  382.8 11.6 %copy-start.26 = (f32[32,128]{1,0:T(8,128)}, f32[32,128]{1,0:T(8,128)S(1)}, u32[]{:S(2)}) copy-start(f32[32,128]{1,0:T(8,128)S(1)} %get-tuple-element.288) | copy-start | bytes 49156
  421.6 17.5 %copy-start.18 = (bf16[64,4096]{1,0:T(8,128)(2,1)S(1)}, bf16[64,4096]{1,0:T(8,128)(2,1)}, u32[]{:S(2)}) copy-start(bf16[64,4096]{1,0:T(8,128)(2,1)} %param.24) | copy-start | bytes 1572868
  421.6 18.4 %copy-start.14 = (bf16[64,4096]{1,0:T(8,128)(2,1)S(1)}, bf16[64,4096]{1,0:T(8,128)(2,1)}, u32[]{:S(2)}) copy-start(bf16[64,4096]{1,0:T(8,128)(2,1)} %param.28) | copy-start | bytes 1572868
  421.6 19.4 %copy-start.21 = (bf16[64,4096]{1,0:T(8,128)(2,1)S(1)}, bf16[64,4096]{1,0:T(8,128)(2,1)}, u32[]{:S(2)}) copy-start(bf16[64,4096]{1,0:T(8,128)(2,1)} %param.27) | copy-start | bytes 1572868
  421.6 257.6 %all-to-all-start.1 = ((bf16[128,64,1024]{2,1,0:T(8,128)(2,1)}), bf16[128,64,1024]{2,1,0:T(8,128)(2,1)}, u32[]{:S(2)}, u32[]{:S(2)}) async-start(bf16[128,64,1024]{2,1,0:T(8,128)(2,1)} %bitcast.294), calls=%async_computation.2 | async-start | bytes 33554432 | tf_op jit(solution)/shard_map/all_to_all | solution.py:182
  438.3 4.0 copy-start.5
  438.3 195.5 %reduce-scatter.2.cloned.1.call-start = ((), (), s32[]{:S(2)}) async-start(), calls=%async_computation.4 | async-start | bytes 3538944 | tf_op jit(solution)/shard_map/reduce_scatter | solution.py:154
  440.0 3.5 copy-start.10
  441.1 5.0 copy-start.29
  453.8 4.4 copy-start.12
  455.1 3.8 copy-start.19
  455.1 3.8 copy-start.20
  455.1 3.8 copy-start.25
  455.1 3.8 copy-start.27
  455.1 3.8 copy-start.31
  456.5 4.0 copy-start.6
  458.9 1.9 copy-start.8
  460.9 1.4 copy-start.13
  474.0 11.0 %copy-start.3 = (f32[4,1024,128,8]{2,1,3,0:T(8,128)}, f32[4,1024,128,8]{2,1,3,0:T(8,128)S(1)}, u32[]{:S(2)}) copy-start(f32[4,1024,128,8]{2,1,3,0:T(8,128)S(1)} %fusion.55) | copy-start | bytes 50331652
  491.9 2.8 copy-start.17
  491.9 2.8 copy-start.22
  492.0 2.8 copy-start.33
  504.7 1.9 copy-start.11
  518.1 6.9 copy-start.7
  534.6 100.9 %copy-start.2 = (f32[128,4096]{0,1:T(8,128)S(1)}, f32[128,4096]{0,1:T(8,128)}, u32[]{:S(2)}) copy-start(f32[128,4096]{0,1:T(8,128)} %get-tuple-element.281) | copy-start | bytes 6291460
Sparse Core Ops, SparseCore 0:
  29.9 178.6 all-gather.1
  525.0 108.7 reduce-scatter.1
where the time goes:
time: 705 us; the launch traced here: 695 us
  waiting for transfers between devices  356 us (50%)
  local copies, waits for them, and re-layouts  129 us (18%)
  matrix products  117 us (17%)
  other arithmetic  49.5 us (7%)
  starting transfers between devices  27.5 us (4%)
  between operations  15 us (2%)
    all_to_all x1, waiting for transfers between devices, shards(): lax.all_to_all(spread.reshape(-1, pair_width), ('pass', 'query'), split_a...  222 us
    reduce_scatter x1, waiting for transfers between devices, shards(): lax.psum_scatter(piece_grads.astype(jnp.bfloat16), 'query', scatter_dimen...  96.1 us
    all_to_all x1, waiting for transfers between devices, shards(): lax.all_to_all(expanded.reshape(-1, pair_width), ('pass', 'query'), split...  38.4 us
    dot_general x10, matrix products, attend_back(): jnp.einsum('qkgd,tkd->kgqt', grad_heads, value_heads, preferred_element_t...  37.7 us
    dot_general x10, matrix products, attend_back(): jnp.einsum('kgqt,qkgd->tkd', weights_low, grad_heads, preferred_element_t...  30.6 us
    scatter x1, local copies, waits for them, and re-layouts, shards(): jnp.zeros((pass_count, passage_span, pair_width), jnp.bfloat16)  21.3 us
    dot_general x10, matrix products, attend_back(): jnp.einsum('kgqt,qkgd->tkd', score_low, query_heads, preferred_element_ty...  19.9 us
    all_to_all x1, starting transfers between devices, shards(): lax.all_to_all(expanded.reshape(-1, pair_width), ('pass', 'query'), split...  16.7 us
  transfers between devices with their start and end apart: 4, of which 3 were waited for; matrix products, arithmetic and copies ran while one was open for 38% of the time, Pallas kernels for 0%

commit v1 on v0

v1 whole, which is shorter than its diff:
```python
import functools
import math

import jax
import jax.numpy as jnp
from jax import lax
from jax.experimental import pallas as pl
from jax.experimental.pallas import tpu as pltpu
from jax.sharding import PartitionSpec as P

H = 32
KVH = 4
HD = 128
GROUP = H // KVH
WIDE = GROUP * HD
QROWS = 128
PROWS = 64
READS = 8
PASSAGES = 16
SCALE = HD ** (-0.5)
LOG2E = math.log2(math.e)
FOLD = SCALE * LOG2E
HIDDEN = -1e30
NT = (((1,), (1,)), ((), ()))
MESH = pl.DeviceIdType.MESH
f32 = jnp.float32
bf16 = jnp.bfloat16


def tile(keys, values, queries, grads, norm, delta, bias=None):
    scores = lax.dot_general(keys, queries, NT, preferred_element_type=f32)
    slopes = lax.dot_general(values, grads, NT, preferred_element_type=f32)
    power = scores * FOLD - norm
    if bias is not None:
        power = power + bias
    weight = jnp.exp2(power)
    score = (weight * (slopes - delta)).astype(bf16)
    weight = weight.astype(bf16)
    dv = jnp.dot(weight, grads, preferred_element_type=f32)
    dk = jnp.dot(score, queries, preferred_element_type=f32)
    dqt = jnp.dot(keys.T, score, preferred_element_type=f32)
    return dk, dv, dqt


def heads_down(ref, *lead):
    return jnp.concatenate([ref[(*lead, slice(None), pl.ds(h * HD, HD))] for h in range(GROUP)], 0)


def heads_along(stat, first):
    return jnp.concatenate([stat[first + h : first + h + 1, :] for h in range(GROUP)], 1)


def body(
    reads, lens,
    q, k, v, out, dout, lse, seg,
    pq, pk, pv, pout, pdout, plse,
    dq_o, dk_o, dv_o, pdq_o, pdk_o, pdv_o,
    out_v, dout_v, pout_v, pdout_v,
    stat, pstat, st, pst,
    qa, da, pqa, pda,
    shard, kv_a, kv_b, bkv, segc,
    dqt, acc_a, acc_b, acc_s, acc_l,
    dqs, pdqs,
    cs_a, cs_b, cr_a, cr_b, ps_a, ps_b, pr_a, pr_b,
    ls_s, ls_r, ss_s, ss_r, fin, fin_s,
    zs, zr, gs, gr, xs, xr, es, er, rs, rr, bs, br, lo,
):
    b = lax.axis_index("pass")
    r = lax.axis_index("query")
    X, Y, Z, K = b // 4, b % 4, r // 2, r % 2
    other = 1 - K

    def zdev(d):
        return (b, ((Z + d) % 4) * 2 + K)

    def pdev(dx, dy):
        return (((X + dx) % 4) * 4 + (Y + dy) % 4, r)

    core = (b, Z * 2 + other)
    plane = [(dx, dy) for dx in range(4) for dy in range(4) if (dx, dy) != (0, 0)]
    halves = (0, 1)
    kv_h, acc_h = (kv_a, kv_b), (acc_a, acc_b)
    cs_h, cr_h, ps_h, pr_h = (cs_a, cs_b), (cr_a, cr_b), (ps_a, ps_b), (pr_a, pr_b)
    pending = []

    def remote(src, dst, s, rcv, to):
        return pltpu.make_async_remote_copy(
            src_ref=src, dst_ref=dst, send_sem=s, recv_sem=rcv, device_id=to, device_id_type=MESH
        )

    def send(*args):
        c = remote(*args)
        c.start()
        pending.append(c)
        return c

    def cols(index, width):
        return pl.ds(pl.multiple_of(index * width, width), width)

    barrier = pltpu.get_barrier_semaphore()
    greet = [zdev(d) for d in (1, 2, 3)] + [pdev(*o) for o in plane] + [core]
    for to in greet:
        pl.semaphore_signal(barrier, inc=1, device_id=to, device_id_type=MESH)
    pl.semaphore_wait(barrier, len(greet))

    def z_out(kind, d, src, dst):
        return send(src, dst, zs.at[kind, d - 1], zr.at[kind, d - 1], zdev(d))

    zc = {}
    for d in (1, 3, 2):
        c = (Z + d) % 4
        zc[0, d] = z_out(0, d, pk.at[:, cols(c, HD)], shard.at[Z, :, 0:HD])
        zc[1, d] = z_out(1, d, pv.at[:, cols(c, HD)], shard.at[Z, :, HD : 2 * HD])
    mine = []

    def local(src, dst):
        c = pltpu.make_async_copy(src, dst, lo.at[len(mine)])
        c.start()
        mine.append(c)
        return c

    own = [
        local(pk.at[:, cols(Z, HD)], shard.at[Z, :, 0:HD]),
        local(pv.at[:, cols(Z, HD)], shard.at[Z, :, HD : 2 * HD]),
    ]
    own_b = [
        local(k.at[:, cols(Z, HD)], bkv.at[Z, K, :, 0:HD]),
        local(v.at[:, cols(Z, HD)], bkv.at[Z, K, :, HD : 2 * HD]),
    ]
    own_q = [
        local(q.at[:, cols(Z, WIDE)], qa.at[0]),
        local(dout.at[:, cols(Z, WIDE)], da.at[0]),
    ]
    own_p = [
        local(pq.at[:, cols(Z, WIDE)], pqa.at[0]),
        local(pdout.at[:, cols(Z, WIDE)], pda.at[0]),
    ]
    own_d = [local(out, out_v), local(dout, dout_v), local(pout, pout_v), local(pdout, pdout_v)]
    for d in (1, 3, 2):
        c = (Z + d) % 4
        zc[2, d] = z_out(2, d, k.at[:, cols(c, HD)], bkv.at[Z, K, :, 0:HD])
        zc[3, d] = z_out(3, d, v.at[:, cols(c, HD)], bkv.at[Z, K, :, HD : 2 * HD])
    for d in (1, 3, 2):
        c = (Z + d) % 4
        zc[4, d] = z_out(4, d, q.at[:, cols(c, WIDE)], qa.at[d])
        zc[5, d] = z_out(5, d, dout.at[:, cols(c, WIDE)], da.at[d])

    for c in own:
        c.wait()
    for d in (1, 3, 2):
        zc[0, d].wait_recv()
        zc[1, d].wait_recv()
    gather = {}
    for half in halves:
        src = shard.at[2 * half : 2 * half + 2]
        dst = kv_h[half].at[b, :, K]
        local(src, dst)
        for i, o in enumerate(plane):
            gather[half, o] = send(src, dst, gs.at[half, i], gr.at[half, i], pdev(*o))
    own_g = mine[-2:]

    for d in (1, 3, 2):
        c = (Z + d) % 4
        zc[6, d] = z_out(6, d, pq.at[:, cols(c, WIDE)], pqa.at[d])
        zc[7, d] = z_out(7, d, pdout.at[:, cols(c, WIDE)], pda.at[d])

    pstat[...] = jnp.zeros_like(pstat)
    for c in own_d:
        c.wait()

    def group_stats(c, _):
        stat[c, 0:GROUP, :] = lse[pl.ds(pl.multiple_of(c * GROUP, GROUP), GROUP), :] * LOG2E
        pstat[c, 0:GROUP, 0:PROWS] = plse[pl.ds(pl.multiple_of(c * GROUP, GROUP), GROUP), :] * LOG2E
        for h in range(GROUP):
            at = pl.ds(pl.multiple_of(c * WIDE + h * HD, HD), HD)
            prod = dout_v[:, at].astype(f32) * out_v[:, at].astype(f32)
            stat[c, GROUP + h : GROUP + h + 1, :] = jnp.sum(prod.T, axis=0, keepdims=True)
            prod = pdout_v[:, at].astype(f32) * pout_v[:, at].astype(f32)
            pstat[c, GROUP + h : GROUP + h + 1, 0:PROWS] = jnp.sum(prod.T, axis=0, keepdims=True)
        return 0

    lax.fori_loop(0, KVH, group_stats, 0)
    for d in (1, 3, 2):
        c = (Z + d) % 4
        zc[8, d] = z_out(8, d, stat.at[c], st.at[d])
        zc[9, d] = z_out(9, d, pstat.at[c], pst.at[d])
    st[0] = stat[Z]
    pst[0] = pstat[Z]

    for ref in (dqt, acc_a, acc_b, acc_s, acc_l):
        ref[...] = jnp.zeros_like(ref)
    for block in range(8):
        row = seg[:, block * 128 : (block + 1) * 128].astype(f32)
        segc[block * 128 : (block + 1) * 128, :] = jnp.broadcast_to(row, (128, 128)).T

    def self_chunk(slot):
        rb = ((Z - slot + 4) % 4) * 2 + K
        first = jnp.clip(rb - 4, 0, 3)
        start = pl.multiple_of(first * 128, 128)
        at = pl.ds(start, 640)
        key_pos = start + lax.broadcasted_iota(jnp.int32, (640, 128), 0)
        row_pos = rb * 128 + lax.broadcasted_iota(jnp.int32, (640, 128), 1)
        row_seg = seg[:, pl.ds(pl.multiple_of(rb * 128, 128), 128)].astype(f32)
        seen = (key_pos <= row_pos) & (segc[at, :] == row_seg)
        bias = jnp.where(seen, 0.0, HIDDEN)
        pairs = [bkv[(first + i) // 2, (first + i) % 2] for i in range(5)]
        pairs = jnp.concatenate(pairs, 0)
        dk, dv, part = tile(
            pairs[:, :HD], pairs[:, HD:], heads_down(qa, slot), heads_down(da, slot),
            heads_along(st[slot], 0), heads_along(st[slot], GROUP),
            jnp.concatenate([bias] * GROUP, 1),
        )
        dqt[slot] += part
        for i in range(5):
            zi, ki = (first + i) // 2, (first + i) % 2
            acc_s[zi, ki, :, :HD] += dk[i * 128 : (i + 1) * 128]
            acc_s[zi, ki, :, HD:] += dv[i * 128 : (i + 1) * 128]

    def cross(half, slot, j):
        p = reads[b, j]
        pairs = kv_h[half][p].reshape(256, 2 * HD)
        if half == 1:
            pos = 256 + lax.broadcasted_iota(jnp.int32, (256, 2 * HD), 0)
            pairs = jnp.where(pos < lens[p], pairs.astype(f32), 0.0).astype(bf16)
        dk, dv, part = tile(
            pairs[:, :HD], pairs[:, HD:], heads_down(qa, slot), heads_down(da, slot),
            heads_along(st[slot], 0), heads_along(st[slot], GROUP),
        )
        dqt[slot] += part
        acc = acc_h[half]
        acc[j, :, :, :, :HD] += dk.reshape(2, 2, 64, HD)
        acc[j, :, :, :, HD:] += dv.reshape(2, 2, 64, HD)

    def cross_all(half, slot):
        def one(j, _):
            cross(half, slot, j)
            return 0
        lax.fori_loop(0, READS, one, 0)

    for c in own_b + own_q:
        c.wait()
    for d in (1, 3, 2):
        zc[2, d].wait_recv()
        zc[3, d].wait_recv()
    fwd = {}

    def forward(half):
        for dx in range(4):
            for dy in range(4):
                if (dx, dy) != (0, 0):
                    gather[half, (dx, dy)].wait_recv()
            at = pl.ds(((X + 4 - dx) % 4) * 4, 4)
            part = kv_h[half].at[at, :, K]
            fwd[half, dx] = send(part, part, xs.at[half, dx], xr.at[half, dx], core)

    bpart = bkv.at[:, K]
    bfwd = send(bpart, bpart, es.at[4], er.at[4], core)
    for c in own_g:
        c.wait()
    bfwd.wait_recv()
    self_chunk(0)
    forward(0)
    for dx in range(4):
        fwd[0, dx].wait_recv()
    cross_all(0, 0)
    forward(1)
    for d in (1, 3):
        for kind in (4, 5, 8):
            zc[kind, d].wait_recv()

    def pair(i, _):
        cross(0, 1 + 2 * (i // READS), i % READS)
        return 0

    lax.fori_loop(0, 2 * READS, pair, 0)
    for kind in (4, 5, 8):
        zc[kind, 2].wait_recv()
    cross_all(0, 2)

    def where_read(p):
        at, has = 0, 0.0
        for j in range(READS):
            hit = reads[b, j] == p
            at = jnp.where(hit, j, at)
            has = jnp.where(hit, 1.0, has)
        return at, has

    def to_core(half):
        acc = acc_h[half]

        def one(p, _):
            at, has = where_read(p)
            cs_h[half][p] = (acc[at, :, other] * has).astype(bf16)
            return 0

        lax.fori_loop(0, PASSAGES, one, 0)
        return send(cs_h[half], cr_h[half], es.at[half], er.at[half], core)

    scattered = {}

    def to_plane(half, moved):
        moved.wait_recv()
        acc = acc_h[half]

        def one(p, _):
            at, has = where_read(p)
            ps_h[half][p] = (acc[at, :, K] * has + cr_h[half][p].astype(f32)).astype(bf16)
            return 0

        lax.fori_loop(0, PASSAGES, one, 0)
        for i, (dx, dy) in enumerate(plane):
            to = pdev(dx, dy)
            scattered[half, i] = send(
                ps_h[half].at[to[0]], pr_h[half].at[i], rs.at[half, i], rr.at[half, i], to
            )

    moved_a = to_core(0)

    for c in own_p:
        c.wait()
    for d in (1, 3, 2):
        for kind in (6, 7, 9):
            zc[kind, d].wait_recv()
    for dx in range(4):
        fwd[1, dx].wait_recv()

    def passage_chunk(step, _):
        s0, s1 = 2 * step, 2 * step + 1
        lane = lax.broadcasted_iota(jnp.int32, (512, 128), 1)
        zrow = jnp.where(lane < PROWS, (Z - s0 + 4) % 4, (Z - s1 + 4) % 4)
        row_pos = (2 * zrow + K) * PROWS + lane % PROWS
        key_pos = lax.broadcasted_iota(jnp.int32, (512, 128), 0)
        seen = (key_pos <= row_pos) & (row_pos < lens[b])
        bias = jnp.where(seen, 0.0, HIDDEN)
        pairs = jnp.concatenate([kv_a[b].reshape(256, 2 * HD), kv_b[b].reshape(256, 2 * HD)], 0)

        def rows(ref):
            parts = []
            for h in range(GROUP):
                parts.append(ref[s0, :, pl.ds(h * HD, HD)])
                parts.append(ref[s1, :, pl.ds(h * HD, HD)])
            return jnp.concatenate(parts, 0)

        stats = jnp.concatenate([pst[s0][:, :PROWS], pst[s1][:, :PROWS]], 1)
        dk, dv, part = tile(
            pairs[:, :HD], pairs[:, HD:], rows(pqa), rows(pda),
            heads_along(stats, 0), heads_along(stats, GROUP),
            jnp.concatenate([bias] * GROUP, 1),
        )
        acc_l[:, :, :, :HD] += dk.reshape(4, 2, PROWS, HD)
        acc_l[:, :, :, HD:] += dv.reshape(4, 2, PROWS, HD)
        for h in range(GROUP):
            block = (part[:, h * HD : (h + 1) * HD] * SCALE).T.astype(bf16)
            pdqs[s0, :, h * HD : (h + 1) * HD] = block[:PROWS]
            pdqs[s1, :, h * HD : (h + 1) * HD] = block[PROWS:]
        return 0

    lax.fori_loop(0, 2, passage_chunk, 0)
    ls_s[...] = acc_l[:, other].astype(bf16)
    moved_l = send(ls_s, ls_r, es.at[2], er.at[2], core)
    to_plane(0, moved_a)
    back = []

    def home(kind, slot, src, dst):
        return remote(src, dst, bs.at[kind, slot - 1], br.at[kind, slot - 1], zdev(4 - slot))

    for slot in (1, 3, 2):
        c = home(1, slot, pdqs.at[slot], pdq_o.at[:, cols(Z, WIDE)])
        c.start()
        back.append(c)
    local(pdqs.at[0], pdq_o.at[:, cols(Z, WIDE)])
    own_out = [mine[-1]]

    def finish_dq(slot):
        for h in range(GROUP):
            at = slice(h * HD, (h + 1) * HD)
            dqs[slot, :, at] = (dqt[slot, :, at] * SCALE).T.astype(bf16)

    def dq_home(slot):
        return home(0, slot, dqs.at[slot], dq_o.at[:, cols(Z, WIDE)])

    def rest(i, _):
        slot = jnp.where(i == 0, 2, 2 * i - 1)
        cross_all(1, slot)
        self_chunk(slot)
        finish_dq(slot)
        dq_home(slot).start()
        return 0

    lax.fori_loop(0, 3, rest, 0)
    ss_s[...] = acc_s[:, other].astype(bf16)
    moved_s = send(ss_s, ss_r, es.at[3], er.at[3], core)
    cross_all(1, 0)
    moved_b = to_core(1)
    finish_dq(0)
    local(dqs.at[0], dq_o.at[:, cols(Z, WIDE)])
    own_out.append(mine[-1])
    scaled = jnp.where(lax.broadcasted_iota(jnp.int32, (1, 2 * HD), 1) < HD, SCALE, 1.0)
    moved_s.wait_recv()
    fin_s[...] = ((acc_s[:, K] + ss_r[...].astype(f32)) * scaled).astype(bf16)
    to_plane(1, moved_b)

    def spread(kind, src, dk, dv):
        for d in (1, 3, 2):
            c = (Z + d) % 4
            for n, o in ((0, dk), (1, dv)):
                back.append(
                    remote(
                        src.at[c, :, n * HD : (n + 1) * HD], o.at[:, cols(Z, HD)],
                        bs.at[kind + n, d - 1], br.at[kind + n, d - 1], zdev(d),
                    )
                )
                back[-1].start()
        for n, o in ((0, dk), (1, dv)):
            own_out.append(local(src.at[Z, :, n * HD : (n + 1) * HD], o.at[:, cols(Z, HD)]))

    spread(2, fin_s, dk_o, dv_o)
    moved_l.wait_recv()
    for half in halves:
        for i in range(len(plane)):
            scattered[half, i].wait_recv()
        at, has = where_read(b)
        total = acc_h[half][at, :, K] * has + cr_h[half][b].astype(f32)
        zz = slice(2 * half, 2 * half + 2)
        total = total + acc_l[zz, K] + ls_r[zz].astype(f32)
        for i in range(len(plane)):
            total = total + pr_h[half][i].astype(f32)
        shape = (2, PROWS, 2 * HD)
        pos = (
            (2 * (lax.broadcasted_iota(jnp.int32, shape, 0) + 2 * half) + K) * PROWS
            + lax.broadcasted_iota(jnp.int32, shape, 1)
        )
        fin[zz] = jnp.where(pos < lens[b], total * scaled, 0.0).astype(bf16)
    spread(4, fin, pdk_o, pdv_o)
    for c in own_out:
        c.wait()
    for c in back:
        c.wait()
    for slot in (1, 2, 3):
        dq_home(slot).wait()
    for c in pending:
        c.wait_send()


def shards(
    query_q, query_k, query_v, query_out, query_dout, query_lse, query_seg,
    passage_q, passage_k, passage_v, passage_out, passage_dout, passage_lse,
    passage_len, reads,
):
    hbm = pl.BlockSpec(memory_space=pl.ANY)
    vmem = pl.BlockSpec(memory_space=pltpu.VMEM)
    smem = pl.BlockSpec(memory_space=pltpu.SMEM)
    pair = 2 * HD
    V = pltpu.VMEM
    dma = pltpu.SemaphoreType.DMA
    wide = H * HD
    half_shape = (PASSAGES, 2, PROWS, pair)
    scratch = [
        V((QROWS, wide), bf16), V((QROWS, wide), bf16), V((PROWS, wide), bf16), V((PROWS, wide), bf16),
        V((KVH, 16, 128), f32), V((KVH, 16, 128), f32), V((4, 16, 128), f32), V((4, 16, 128), f32),
        V((4, QROWS, WIDE), bf16), V((4, QROWS, WIDE), bf16),
        V((4, PROWS, WIDE), bf16), V((4, PROWS, WIDE), bf16),
        V((4, PROWS, pair), bf16),
        V((PASSAGES, 2, 2, PROWS, pair), bf16), V((PASSAGES, 2, 2, PROWS, pair), bf16),
        V((4, 2, QROWS, pair), bf16), V((1024, 128), f32),
        V((4, HD, WIDE), f32),
        V((READS, 2, 2, PROWS, pair), f32), V((READS, 2, 2, PROWS, pair), f32),
        V((4, 2, QROWS, pair), f32), V((4, 2, PROWS, pair), f32),
        V((4, QROWS, WIDE), bf16), V((4, PROWS, WIDE), bf16),
        V(half_shape, bf16), V(half_shape, bf16), V(half_shape, bf16), V(half_shape, bf16),
        V(half_shape, bf16), V(half_shape, bf16),
        V((15, 2, PROWS, pair), bf16), V((15, 2, PROWS, pair), bf16),
        V((4, PROWS, pair), bf16), V((4, PROWS, pair), bf16),
        V((4, QROWS, pair), bf16), V((4, QROWS, pair), bf16),
        V((4, PROWS, pair), bf16), V((4, QROWS, pair), bf16),
        dma((10, 3)), dma((10, 3)), dma((2, 15)), dma((2, 15)), dma((2, 4)), dma((2, 4)),
        dma((5,)), dma((5,)), dma((2, 15)), dma((2, 15)), dma((6, 3)), dma((6, 3)), dma((24,)),
    ]
    shape = jax.ShapeDtypeStruct
    return pl.pallas_call(
        body,
        out_shape=(
            shape((QROWS, wide), bf16), shape((QROWS, KVH * HD), bf16), shape((QROWS, KVH * HD), bf16),
            shape((PROWS, wide), bf16), shape((PROWS, KVH * HD), bf16), shape((PROWS, KVH * HD), bf16),
        ),
        in_specs=[smem, smem, hbm, hbm, hbm, hbm, hbm, vmem, vmem, hbm, hbm, hbm, hbm, hbm, vmem],
        out_specs=(hbm,) * 6,
        scratch_shapes=scratch,
        compiler_params=pltpu.CompilerParams(
            collective_id=0, has_side_effects=True, vmem_limit_bytes=60 * 2**20
        ),
    )(
        reads, passage_len,
        query_q, query_k, query_v, query_out, query_dout, query_lse, query_seg,
        passage_q, passage_k, passage_v, passage_out, passage_dout, passage_lse,
    )


def solution(mesh):
    rows = P(("pass", "query"), None)
    along = P(None, ("pass", "query"))
    return jax.shard_map(
        shards,
        mesh=mesh,
        in_specs=(
            rows, rows, rows, rows, rows, along, P("pass", None),
            rows, rows, rows, rows, rows, along, P(), P(),
        ),
        out_specs=(rows,) * 6,
        check_vma=False,
    )
```

time: 705 us -> 140 us (0.20)
  the two profiles are of different devices: /device:TPU:50 before, /device:TPU:1 now
where the time goes in v1:
time: 140 us; the launch traced here: 139 us
  Pallas kernels  131 us (94%)
  local copies, waits for them, and re-layouts  7.67 us (5%)
    pallas_call x1, Pallas kernels, shards(): pl.pallas_call(body, out_shape=(shape((QROWS, wide), bf16), shape((QROWS,...  131 us
    unnamed x17, local copies, waits for them, and re-layouts  7.67 us

profile of v1, /device:TPU:1, one launch (start us, length us, event | category | flops | bytes accessed | tf_op | source)
XLA Modules:
  0.0 139.3 jit_solution(14929937120233454143)
XLA Ops:
  0.6 1.4 copy.21.reads
  2.0 131.0 %shard_map.190 = (bf16[128,4096]{1,0:T(8,128)(2,1)}, bf16[128,512]{1,0:T(8,128)(2,1)}, bf16[128,512]{1,0:T(8,128)(2,1)}, bf16[64,4096]{1,0:T(8,128)(2,1)}, bf16[...) custom-call(s32[16,8]{1,0:T(8,128)} %copy.21.reads, s32[16]{0:T(128)} %lens.1, bf16[128,4096]{1,0:T(8,128)(2,1)} %q.1, ...), custom_call_target="tpu_custom_call" | custom-call | tf_op jit(solution)/shard_map/pallas_call | solution.py:480
  132.9 0.0 copy-start.2
  133.0 0.0 copy-start
  133.0 2.4 %copy.28 = bf16[128,4096]{1,0:T(8,128)(2,1)} copy(bf16[128,4096]{1,0:T(8,128)(2,1)} %get-tuple-element.12) | data formatting | bytes 2097152
  135.3 0.0 copy-done.2
  135.3 0.0 copy-start.1
  135.3 0.7 copy.29
  136.0 0.3 copy-done.1
  136.3 0.7 copy.30
  136.9 0.0 copy-done
  136.9 0.0 copy-start.4
  136.9 0.8 copy.31
  137.7 0.1 copy-done.4
  137.8 0.0 copy-start.3
  137.8 0.6 copy.32
  138.4 0.2 copy-done.3
  138.7 0.6 copy.33
Async XLA Ops:
  132.9 2.4 %copy-start.2 = (bf16[128,512]{1,0:T(8,128)(2,1)S(1)}, bf16[128,512]{1,0:T(8,128)(2,1)}, u32[]{:S(2)}) copy-start(bf16[128,512]{1,0:T(8,128)(2,1)} %get-tuple-element.13) | copy-start | bytes 393220
  133.0 4.0 %copy-start = (bf16[64,4096]{1,0:T(8,128)(2,1)S(1)}, bf16[64,4096]{1,0:T(8,128)(2,1)}, u32[]{:S(2)}) copy-start(bf16[64,4096]{1,0:T(8,128)(2,1)} %get-tuple-element.15) | copy-start | bytes 1572868
  135.3 1.0 copy-start.1
  136.9 0.9 copy-start.4
  137.8 0.9 copy-start.3

commit v2 on v1

v2 whole, which is shorter than its diff:
```python
import functools
import math

import jax
import jax.numpy as jnp
from jax import lax
from jax.experimental import pallas as pl
from jax.experimental.pallas import tpu as pltpu
from jax.sharding import PartitionSpec as P

H = 32
KVH = 4
HD = 128
GROUP = H // KVH
WIDE = GROUP * HD
QROWS = 128
PROWS = 64
READS = 8
PASSAGES = 16
UNIT = 32
PARTS = ((0, 2), (2, 3), (5, 2), (7, 1))
RUNS = (
    ((0, 0, 64),),
    ((1, 0, 64), (2, 0, 32)),
    ((2, 32, 32), (3, 0, 32)),
    ((3, 32, 32),),
)
SCALE = HD ** (-0.5)
LOG2E = math.log2(math.e)
FOLD = SCALE * LOG2E
HIDDEN = -1e30
NT = (((1,), (1,)), ((), ()))
MESH = pl.DeviceIdType.MESH
f32 = jnp.float32
bf16 = jnp.bfloat16


def tile(keys, values, queries, grads, norm, delta, bias=None):
    scores = lax.dot_general(keys, queries, NT, preferred_element_type=f32)
    slopes = lax.dot_general(values, grads, NT, preferred_element_type=f32)
    power = scores * FOLD - norm
    if bias is not None:
        power = power + bias
    weight = jnp.exp2(power)
    score = (weight * (slopes - delta)).astype(bf16)
    weight = weight.astype(bf16)
    dv = jnp.dot(weight, grads, preferred_element_type=f32)
    dk = jnp.dot(score, queries, preferred_element_type=f32)
    dqt = jnp.dot(keys.T, score, preferred_element_type=f32)
    return dk, dv, dqt


def heads_down(ref, *lead):
    return jnp.concatenate([ref[(*lead, slice(None), pl.ds(h * HD, HD))] for h in range(GROUP)], 0)


def heads_along(stat, first):
    return jnp.concatenate([stat[first + h : first + h + 1, :] for h in range(GROUP)], 1)


def body(
    reads, lens,
    q, k, v, out, dout, lse, seg,
    pq, pk, pv, pout, pdout, plse,
    dq_o, dk_o, dv_o, pdq_o, pdk_o, pdv_o,
    out_v, dout_v, pout_v, pdout_v,
    stat, pstat, st, pst,
    qa, da, pqa, pda,
    pkv, shard, kv, bkv, segc,
    dqt, acc, acc_s, acc_l,
    dqs, pdqs,
    to_c, from_c, to_p, from_p,
    ls_s, ls_r, ss_s, ss_r, fin, fin_s,
    zs, zr, gs, gr, xs, xr, es, er, rs, rr, bs, br, us, ur, lo,
):
    b = lax.axis_index("pass")
    r = lax.axis_index("query")
    X, Y, Z, K = b // 4, b % 4, r // 2, r % 2
    other = 1 - K
    core = (b, Z * 2 + other)
    plane = [(dx, dy) for dx in range(4) for dy in range(4) if (dx, dy) != (0, 0)]
    pending = []
    mine = []

    def zdev(d):
        return (b, ((Z + d) % 4) * 2 + K)

    def pdev(dx, dy):
        return (((X + dx) % 4) * 4 + (Y + dy) % 4, r)

    def remote(src, dst, s, rcv, to):
        return pltpu.make_async_remote_copy(
            src_ref=src, dst_ref=dst, send_sem=s, recv_sem=rcv, device_id=to, device_id_type=MESH
        )

    def send(*args):
        c = remote(*args)
        c.start()
        pending.append(c)
        return c

    def local(src, dst):
        c = pltpu.make_async_copy(src, dst, lo.at[len(mine)])
        c.start()
        mine.append(c)
        return c

    def cols(index, width):
        return pl.ds(pl.multiple_of(index * width, width), width)

    barrier = pltpu.get_barrier_semaphore()
    greet = [zdev(d) for d in (1, 2, 3)] + [pdev(*o) for o in plane] + [core]
    for to in greet:
        pl.semaphore_signal(barrier, inc=1, device_id=to, device_id_type=MESH)
    held = [
        local(o.at[i * UNIT : (i + 1) * UNIT], pkv.at[i, :, n * KVH * HD : (n + 1) * KVH * HD])
        for n, o in ((0, pk), (1, pv))
        for i in (0, 1)
    ]
    own_d = [local(out, out_v), local(dout, dout_v), local(pout, pout_v), local(pdout, pdout_v)]
    own_q = [
        local(k.at[:, cols(Z, HD)], bkv.at[Z, K, :, 0:HD]),
        local(v.at[:, cols(Z, HD)], bkv.at[Z, K, :, HD : 2 * HD]),
        local(q.at[:, cols(Z, WIDE)], qa.at[0]),
        local(dout.at[:, cols(Z, WIDE)], da.at[0]),
    ]
    own_p = [
        local(pq.at[:, cols(Z, WIDE)], pqa.at[0]),
        local(pdout.at[:, cols(Z, WIDE)], pda.at[0]),
    ]

    for block in range(8):
        row = seg[:, block * 128 : (block + 1) * 128].astype(f32)
        segc[block * 128 : (block + 1) * 128, :] = jnp.broadcast_to(row, (128, 128)).T
    for c in held:
        c.wait()
    shard[pl.ds(2 * Z, 2), :, 0:HD] = pkv[:, :, cols(Z, HD)]
    shard[pl.ds(2 * Z, 2), :, HD : 2 * HD] = pkv[:, :, cols(KVH + Z, HD)]
    pl.semaphore_wait(barrier, len(greet))

    def z_copy(kind, d):
        c = (Z + d) % 4
        src, dst = (
            (pkv.at[:, :, cols(c, HD)], shard.at[pl.ds(2 * Z, 2), :, 0:HD]),
            (pkv.at[:, :, cols(KVH + c, HD)], shard.at[pl.ds(2 * Z, 2), :, HD : 2 * HD]),
            (k.at[:, cols(c, HD)], bkv.at[Z, K, :, 0:HD]),
            (v.at[:, cols(c, HD)], bkv.at[Z, K, :, HD : 2 * HD]),
            (q.at[:, cols(c, WIDE)], qa.at[d]),
            (dout.at[:, cols(c, WIDE)], da.at[d]),
            (pq.at[:, cols(c, WIDE)], pqa.at[d]),
            (pdout.at[:, cols(c, WIDE)], pda.at[d]),
            (stat.at[c], st.at[d]),
            (pstat.at[c], pst.at[d]),
        )[kind]
        return remote(src, dst, zs.at[kind, d - 1], zr.at[kind, d - 1], zdev(d))

    def z_out(kinds, offsets):
        for d in offsets:
            for kind in kinds:
                c = z_copy(kind, d)
                c.start()
                pending.append(c)

    def z_in(kinds, offsets):
        for d in offsets:
            for kind in kinds:
                z_copy(kind, d).wait_recv()

    z_out((0, 1), (1, 3, 2))
    z_out((2, 3), (1, 3, 2))

    z_in((0, 1), (1, 3, 2))
    gather, own_g = {}, {}

    def plane_out(n):
        first, count = PARTS[n]
        src = shard.at[first : first + count]
        dst = kv[n].at[b, :, K]
        own_g[n] = local(src, dst)
        for i, o in enumerate(plane):
            gather[n, o] = send(src, dst, gs.at[n, i], gr.at[n, i], pdev(*o))

    fwd = {}

    def forward(n):
        own_g[n].wait()
        for dx in range(4):
            for dy in range(4):
                if (dx, dy) != (0, 0):
                    gather[n, (dx, dy)].wait_recv()
            at = pl.ds(((X + 4 - dx) % 4) * 4, 4)
            part = kv[n].at[at, :, K]
            fwd[n, dx] = send(part, part, xs.at[n, dx], xr.at[n, dx], core)

    def forwarded(n):
        for dx in range(4):
            fwd[n, dx].wait_recv()

    plane_out(0)
    z_out((4, 5), (1, 3))
    pstat[...] = jnp.zeros_like(pstat)
    for c in own_d:
        c.wait()

    def group_stats(c, _):
        at8 = pl.ds(pl.multiple_of(c * GROUP, GROUP), GROUP)
        stat[c, 0:GROUP, :] = lse[at8, :] * LOG2E
        pstat[c, 0:GROUP, 0:PROWS] = plse[at8, :] * LOG2E
        for h in range(GROUP):
            at = pl.ds(pl.multiple_of(c * WIDE + h * HD, HD), HD)
            prod = dout_v[:, at].astype(f32) * out_v[:, at].astype(f32)
            stat[c, GROUP + h : GROUP + h + 1, :] = jnp.sum(prod.T, axis=0, keepdims=True)
            prod = pdout_v[:, at].astype(f32) * pout_v[:, at].astype(f32)
            pstat[c, GROUP + h : GROUP + h + 1, 0:PROWS] = jnp.sum(prod.T, axis=0, keepdims=True)
        return 0

    lax.fori_loop(0, KVH, group_stats, 0)
    st[0] = stat[Z]
    pst[0] = pstat[Z]
    z_out((8, 9), (1, 3, 2))
    for ref in (dqt, *acc, acc_s, acc_l):
        ref[...] = jnp.zeros_like(ref)

    for c in own_q:
        c.wait()
    z_in((2, 3), (1, 3, 2))
    part = bkv.at[:, K]
    bfwd = send(part, part, es.at[5], er.at[5], core)
    plane_out(1)

    def self_chunk(slot):
        rb = ((Z - slot + 4) % 4) * 2 + K
        first = jnp.clip(rb - 4, 0, 3)
        start = pl.multiple_of(first * 128, 128)
        at = pl.ds(start, 640)
        key_pos = start + lax.broadcasted_iota(jnp.int32, (640, 128), 0)
        row_pos = rb * 128 + lax.broadcasted_iota(jnp.int32, (640, 128), 1)
        row_seg = seg[:, pl.ds(pl.multiple_of(rb * 128, 128), 128)].astype(f32)
        seen = (key_pos <= row_pos) & (segc[at, :] == row_seg)
        bias = jnp.where(seen, 0.0, HIDDEN)
        pairs = jnp.concatenate([bkv[(first + i) // 2, (first + i) % 2] for i in range(5)], 0)
        dk, dv, part = tile(
            pairs[:, :HD], pairs[:, HD:], heads_down(qa, slot), heads_down(da, slot),
            heads_along(st[slot], 0), heads_along(st[slot], GROUP),
            jnp.concatenate([bias] * GROUP, 1),
        )
        dqt[slot] += part
        for i in range(5):
            zi, ki = (first + i) // 2, (first + i) % 2
            acc_s[zi, ki, :, :HD] += dk[i * 128 : (i + 1) * 128]
            acc_s[zi, ki, :, HD:] += dv[i * 128 : (i + 1) * 128]

    def places(first, shape):
        row = lax.broadcasted_iota(jnp.int32, shape, 0)
        unit = first + row // (2 * UNIT)
        return unit // 2 * 128 + row // UNIT % 2 * 64 + unit % 2 * UNIT + row % UNIT

    def cross(n, slot):
        first, count = PARTS[n]
        rows = count * 2 * UNIT
        abreast = -(-256 // rows)

        def one(t, _):
            pairs = []
            for i in range(abreast):
                p = reads[t * abreast + i, b]
                pair = kv[n][p].reshape(rows, 2 * HD)
                if first + count > 6:
                    seen = places(first, (rows, 2 * HD)) < lens[p]
                    pair = jnp.where(seen, pair.astype(f32), 0.0).astype(bf16)
                pairs.append(pair)
            pairs = jnp.concatenate(pairs, 0)
            dk, dv, part = tile(
                pairs[:, :HD], pairs[:, HD:], heads_down(qa, slot), heads_down(da, slot),
                heads_along(st[slot], 0), heads_along(st[slot], GROUP),
            )
            dqt[slot] += part
            at = pl.ds(t * abreast, abreast)
            acc[n][at, :, :, :, :HD] += dk.reshape(abreast, count, 2, UNIT, HD)
            acc[n][at, :, :, :, HD:] += dv.reshape(abreast, count, 2, UNIT, HD)
            return 0

        lax.fori_loop(0, READS // abreast, one, 0)

    def where_read(p):
        at, has = 0, 0.0
        for j in range(READS):
            hit = reads[j, b] == p
            at = jnp.where(hit, j, at)
            has = jnp.where(hit, 1.0, has)
        return at, has

    moved = {}

    def to_core(n):
        def one(p, _):
            at, has = where_read(p)
            to_c[n][p] = (acc[n][at, :, other] * has).astype(bf16)
            return 0

        lax.fori_loop(0, PASSAGES, one, 0)
        moved[n] = send(to_c[n], from_c[n], es.at[n], er.at[n], core)

    scattered = {}

    def to_plane(n):
        moved[n].wait_recv()

        def one(p, _):
            at, has = where_read(p)
            to_p[n][p] = (acc[n][at, :, K] * has + from_c[n][p].astype(f32)).astype(bf16)
            return 0

        lax.fori_loop(0, PASSAGES, one, 0)
        for i, (dx, dy) in enumerate(plane):
            to = pdev(dx, dy)
            scattered[n, i] = send(
                to_p[n].at[to[0]], from_p[n].at[i], rs.at[n, i], rr.at[n, i], to
            )

    def passage_chunk(step, _):
        s0, s1 = 2 * step, 2 * step + 1
        lane = lax.broadcasted_iota(jnp.int32, (512, 128), 1)
        zrow = jnp.where(lane < PROWS, (Z - s0 + 4) % 4, (Z - s1 + 4) % 4)
        row_pos = (2 * zrow + K) * PROWS + lane % PROWS
        key_pos = places(0, (512, 128))
        seen = (key_pos <= row_pos) & (row_pos < lens[b])
        bias = jnp.where(seen, 0.0, HIDDEN)
        pairs = jnp.concatenate([ref[b].reshape(-1, 2 * HD) for ref in kv], 0)

        def rows(ref):
            parts = []
            for h in range(GROUP):
                parts.append(ref[s0, :, pl.ds(h * HD, HD)])
                parts.append(ref[s1, :, pl.ds(h * HD, HD)])
            return jnp.concatenate(parts, 0)

        stats = jnp.concatenate([pst[s0][:, :PROWS], pst[s1][:, :PROWS]], 1)
        dk, dv, part = tile(
            pairs[:, :HD], pairs[:, HD:], rows(pqa), rows(pda),
            heads_along(stats, 0), heads_along(stats, GROUP),
            jnp.concatenate([bias] * GROUP, 1),
        )
        acc_l[:, :, :, :HD] += dk.reshape(8, 2, UNIT, HD)
        acc_l[:, :, :, HD:] += dv.reshape(8, 2, UNIT, HD)
        for h in range(GROUP):
            block = (part[:, h * HD : (h + 1) * HD] * SCALE).T.astype(bf16)
            pdqs[s0, :, h * HD : (h + 1) * HD] = block[:PROWS]
            pdqs[s1, :, h * HD : (h + 1) * HD] = block[PROWS:]
        return 0

    def home(kind, slot, src, dst):
        return remote(src, dst, bs.at[kind, slot - 1], br.at[kind, slot - 1], zdev(4 - slot))

    def finish_dq(slot):
        for h in range(GROUP):
            at = slice(h * HD, (h + 1) * HD)
            dqs[slot, :, at] = (dqt[slot, :, at] * SCALE).T.astype(bf16)

    def dq_home(slot):
        return home(0, slot, dqs.at[slot], dq_o.at[:, cols(Z, WIDE)])

    back, own_out = [], []

    def spread(kind, src, dk, dv):
        for d in (1, 3, 2):
            c = (Z + d) % 4
            for n, o in ((0, dk), (1, dv)):
                back.append(
                    remote(
                        src.at[c, :, n * HD : (n + 1) * HD], o.at[:, cols(Z, HD)],
                        bs.at[kind + n, d - 1], br.at[kind + n, d - 1], zdev(d),
                    )
                )
                back[-1].start()
        for n, o in ((0, dk), (1, dv)):
            own_out.append(local(src.at[Z, :, n * HD : (n + 1) * HD], o.at[:, cols(Z, HD)]))

    scaled = jnp.where(lax.broadcasted_iota(jnp.int32, (1, 2 * HD), 1) < HD, SCALE, 1.0)
    runs = [(n, run) for n in range(len(PARTS)) for run in RUNS[n]]

    def run_copy(i, which):
        chip, row, rows = runs[i][1]
        src = fin.at[chip, row : row + rows, which * HD : (which + 1) * HD]
        dst = (pdk_o, pdv_o)[which].at[row : row + rows, cols(Z, HD)]
        return src, dst, chip

    def run_remote(i, which, d):
        src, dst, chip = run_copy(i, which)
        at = 2 * i + which
        return remote(src, dst, us.at[at, d - 1], ur.at[at, d - 1], (b, chip * 2 + K))

    def run_local(i, which):
        src, dst, chip = run_copy(i, which)
        return pltpu.make_async_copy(src, dst, us.at[2 * i + which, 3])

    def final(n):
        first, count = PARTS[n]
        for i in range(len(plane)):
            scattered[n, i].wait_recv()
        at, has = where_read(b)
        units = slice(first, first + count)
        total = acc[n][at, :, K] * has + from_c[n][b].astype(f32)
        total = total + acc_l[units, K] + ls_r[units].astype(f32)
        for i in range(len(plane)):
            total = total + from_p[n][i].astype(f32)
        total = total * scaled
        for u in range(count):
            chip, row = (first + u) // 2, (first + u) % 2 * UNIT
            pos = chip * 128 + K * 64 + row
            pos = pos + lax.broadcasted_iota(jnp.int32, (UNIT, 2 * HD), 0)
            fin[chip, row : row + UNIT, :] = jnp.where(pos < lens[b], total[u], 0.0).astype(bf16)
        for i, (part, (chip, _, _)) in enumerate(runs):
            if part == n:
                @pl.when(Z != chip)
                def _():
                    for which in (0, 1):
                        run_remote(i, which, (chip - Z + 4) % 4).start()

                @pl.when(Z == chip)
                def _():
                    for which in (0, 1):
                        run_local(i, which).start()

    def finals_done():
        for i, (_, (chip, _, _)) in enumerate(runs):
            @pl.when(Z != chip)
            def _():
                for which in (0, 1):
                    run_remote(i, which, (chip - Z + 4) % 4).wait_send()

            @pl.when(Z == chip)
            def _():
                for which in (0, 1):
                    run_local(i, which).wait()
                    for d in (1, 2, 3):
                        run_remote(i, which, d).wait_recv()

    def chunks(n, slots):
        count, slot_of = slots

        def one(i, _):
            cross(n, slot_of(i))
            return 0

        lax.fori_loop(0, count, one, 0)

    forward(0)
    z_out((4, 5), (2,))
    bfwd.wait_recv()
    self_chunk(0)
    forwarded(0)
    cross(0, 0)
    z_in((4, 5, 8), (1, 3))
    chunks(0, (2, lambda i: 1 + 2 * i))

    def self_near(i, _):
        self_chunk(1 + 2 * i)
        return 0

    lax.fori_loop(0, 2, self_near, 0)
    forward(1)
    plane_out(2)
    forwarded(1)
    cross(1, 0)
    z_in((4, 5, 8), (2,))
    z_out((6, 7), (1, 3, 2))
    cross(0, 2)
    to_core(0)
    cross(1, 1)
    to_plane(0)
    chunks(1, (2, lambda i: 3 - i))
    to_core(1)
    self_chunk(2)
    forward(2)
    plane_out(3)
    forwarded(2)
    cross(2, 0)
    to_plane(1)
    chunks(2, (3, lambda i: i + 1))
    to_core(2)
    forward(3)
    for c in own_p:
        c.wait()
    z_in((6, 7, 9), (1, 3, 2))
    forwarded(3)
    lax.fori_loop(0, 2, passage_chunk, 0)
    to_plane(2)
    for slot in (1, 3, 2):
        c = home(1, slot, pdqs.at[slot], pdq_o.at[:, cols(Z, WIDE)])
        c.start()
        back.append(c)
    own_out.append(local(pdqs.at[0], pdq_o.at[:, cols(Z, WIDE)]))
    ls_s[...] = acc_l[:, other].astype(bf16)
    moved_l = send(ls_s, ls_r, es.at[6], er.at[6], core)
    ss_s[...] = acc_s[:, other].astype(bf16)
    moved_s = send(ss_s, ss_r, es.at[4], er.at[4], core)

    def last_part(i, _):
        slot = jnp.where(i == 0, 2, 2 * i - 1)
        cross(3, slot)
        finish_dq(slot)
        dq_home(slot).start()
        return 0

    lax.fori_loop(0, 3, last_part, 0)
    cross(3, 0)
    to_core(3)
    finish_dq(0)
    own_out.append(local(dqs.at[0], dq_o.at[:, cols(Z, WIDE)]))
    moved_l.wait_recv()
    final(0)
    to_plane(3)
    moved_s.wait_recv()
    fin_s[...] = ((acc_s[:, K] + ss_r[...].astype(f32)) * scaled).astype(bf16)
    spread(2, fin_s, dk_o, dv_o)
    final(1)
    final(2)
    final(3)
    finals_done()
    for c in own_out:
        c.wait()
    for c in back:
        c.wait()
    for slot in (1, 2, 3):
        dq_home(slot).wait()
    for c in pending:
        c.wait_send()


def place(*refs):
    count = (len(refs) - 1) // 3
    ins, outs, held, sems = refs[:count], refs[count : 2 * count], refs[2 * count : -1], refs[-1]
    there = [pltpu.make_async_copy(ins[i], held[i], sems.at[0, i]) for i in range(count)]
    away = [pltpu.make_async_copy(held[i], outs[i], sems.at[1, i]) for i in range(count)]
    for c in there:
        c.start()
    for i in range(count):
        there[i].wait()
        away[i].start()
    for c in away:
        c.wait()


def shards(
    query_q, query_k, query_v, query_out, query_dout, query_lse, query_seg,
    passage_q, passage_k, passage_v, passage_out, passage_dout, passage_lse,
    passage_len, reads,
):
    hbm = pl.BlockSpec(memory_space=pl.ANY)
    vmem = pl.BlockSpec(memory_space=pltpu.VMEM)
    smem = pl.BlockSpec(memory_space=pltpu.SMEM)
    pair = 2 * HD
    V = pltpu.VMEM
    dma = pltpu.SemaphoreType.DMA
    wide = H * HD
    counts = [count for _, count in PARTS]
    parts = len(counts)
    stats = V((4, 16, 128), f32)
    scratch = [
        V((QROWS, wide), bf16), V((QROWS, wide), bf16), V((PROWS, wide), bf16), V((PROWS, wide), bf16),
        stats, stats, stats, stats,
        V((4, QROWS, WIDE), bf16), V((4, QROWS, WIDE), bf16),
        V((4, PROWS, WIDE), bf16), V((4, PROWS, WIDE), bf16),
        V((2, UNIT, 2 * KVH * HD), bf16), V((8, UNIT, pair), bf16),
        [V((PASSAGES, n, 2, UNIT, pair), bf16) for n in counts],
        V((4, 2, QROWS, pair), bf16), V((1024, 128), f32),
        V((4, HD, WIDE), f32),
        [V((READS, n, 2, UNIT, pair), f32) for n in counts],
        V((4, 2, QROWS, pair), f32), V((8, 2, UNIT, pair), f32),
        V((4, QROWS, WIDE), bf16), V((4, PROWS, WIDE), bf16),
        [V((PASSAGES, n, UNIT, pair), bf16) for n in counts],
        [V((PASSAGES, n, UNIT, pair), bf16) for n in counts],
        [V((PASSAGES, n, UNIT, pair), bf16) for n in counts],
        [V((PASSAGES - 1, n, UNIT, pair), bf16) for n in counts],
        V((8, UNIT, pair), bf16), V((8, UNIT, pair), bf16),
        V((4, QROWS, pair), bf16), V((4, QROWS, pair), bf16),
        V((4, PROWS, pair), bf16), V((4, QROWS, pair), bf16),
        dma((10, 3)), dma((10, 3)), dma((parts, 15)), dma((parts, 15)),
        dma((parts, 4)), dma((parts, 4)),
        dma((7,)), dma((7,)), dma((parts, 15)), dma((parts, 15)), dma((4, 3)), dma((4, 3)),
        dma((12, 4)), dma((12, 3)), dma((24,)),
    ]
    shape = jax.ShapeDtypeStruct
    results = (
        shape((QROWS, wide), bf16), shape((QROWS, KVH * HD), bf16), shape((QROWS, KVH * HD), bf16),
        shape((PROWS, wide), bf16), shape((PROWS, KVH * HD), bf16), shape((PROWS, KVH * HD), bf16),
    )
    found = pl.pallas_call(
        body,
        out_shape=results,
        in_specs=[smem, smem, hbm, hbm, hbm, hbm, hbm, vmem, vmem, hbm, hbm, hbm, hbm, hbm, vmem],
        out_specs=(hbm,) * 6,
        scratch_shapes=scratch,
        compiler_params=pltpu.CompilerParams(
            collective_id=0, has_side_effects=True, vmem_limit_bytes=60 * 2**20
        ),
    )(
        reads.T, passage_len,
        query_q, query_k, query_v, query_out, query_dout, query_lse, query_seg,
        passage_q, passage_k, passage_v, passage_out, passage_dout, passage_lse,
    )
    return pl.pallas_call(
        place,
        out_shape=results,
        in_specs=[hbm] * 6,
        out_specs=(hbm,) * 6,
        scratch_shapes=[V(x.shape, bf16) for x in results] + [dma((2, 6))],
    )(*found)


def solution(mesh):
    rows = P(("pass", "query"), None)
    along = P(None, ("pass", "query"))
    return jax.shard_map(
        shards,
        mesh=mesh,
        in_specs=(
            rows, rows, rows, rows, rows, along, P("pass", None),
            rows, rows, rows, rows, rows, along, P(), P(),
        ),
        out_specs=(rows,) * 6,
        check_vma=False,
    )
```

time: 140 us -> 119 us (0.85)
  Pallas kernels: 131 us -> 118 us
  local copies, waits for them, and re-layouts: 7.67 us -> 0 us
    pallas_call x1 -> x2, Pallas kernels: 131 us -> 118 us  [the longest x1 115 us: shards(): pl.pallas_call(body, out_shape=results, in_specs=[smem, smem, hbm, hbm, h...]
    unnamed x17 -> x0, local copies, waits for them, and re-layouts: 7.67 us -> none
where the time goes in v2:
time: 119 us; the launch traced here: 118 us
  Pallas kernels  118 us (99%)
    pallas_call x1, Pallas kernels, shards(): pl.pallas_call(body, out_shape=results, in_specs=[smem, smem, hbm, hbm, h...  115 us
    pallas_call x1, Pallas kernels, shards(): pl.pallas_call(place, out_shape=results, in_specs=[hbm] * 6, out_specs=(h...  2.59 us

profile of v2, /device:TPU:1, one launch (start us, length us, event | category | flops | bytes accessed | tf_op | source)
XLA Modules:
  0.0 118.4 jit_solution(14555540776422503277)
XLA Ops:
  0.6 115.0 %shard_map.190 = (bf16[128,4096]{1,0:T(8,128)(2,1)}, bf16[128,512]{1,0:T(8,128)(2,1)}, bf16[128,512]{1,0:T(8,128)(2,1)}, bf16[64,4096]{1,0:T(8,128)(2,1)}, bf16[...) custom-call(s32[8,16]{1,0:T(8,128)} %bitcast.1, s32[16]{0:T(128)} %lens.1, bf16[128,4096]{1,0:T(8,128)(2,1)} %q.1, ...), custom_call_target="tpu_custom_call" | custom-call | tf_op jit(solution)/shard_map/pallas_call | solution.py:589
  115.7 2.6 %shard_map.191 = (bf16[128,4096]{1,0:T(8,128)(2,1)}, bf16[128,512]{1,0:T(8,128)(2,1)}, bf16[128,512]{1,0:T(8,128)(2,1)}, bf16[64,4096]{1,0:T(8,128)(2,1)}, bf16[...) custom-call(bf16[128,4096]{1,0:T(8,128)(2,1)} %get-tuple-element.12.refs_0_, bf16[128,512]{1,0:T(8,128)(2,1)} %get-tuple-element.13.refs_1_, ...), custom_call_target="tpu_custom_call" | custom-call | tf_op jit(solution)/shard_map/pallas_call | solution.py:603

commit v3 on v2

--- a/solution.py
+++ b/solution.py
@@ -298,7 +298,7 @@
             to_c[n][p] = (acc[n][at, :, other] * has).astype(bf16)
             return 0
 
-        lax.fori_loop(0, PASSAGES, one, 0)
+        lax.fori_loop(0, PASSAGES, one, 0, unroll=4)
         moved[n] = send(to_c[n], from_c[n], es.at[n], er.at[n], core)
 
     scattered = {}
@@ -311,7 +311,7 @@
             to_p[n][p] = (acc[n][at, :, K] * has + from_c[n][p].astype(f32)).astype(bf16)
             return 0
 
-        lax.fori_loop(0, PASSAGES, one, 0)
+        lax.fori_loop(0, PASSAGES, one, 0, unroll=4)
         for i, (dx, dy) in enumerate(plane):
             to = pdev(dx, dy)
             scattered[n, i] = send(
@@ -454,13 +454,10 @@
     z_in((4, 5, 8), (1, 3))
     chunks(0, (2, lambda i: 1 + 2 * i))
 
-    def self_near(i, _):
-        self_chunk(1 + 2 * i)
-        return 0
-
-    lax.fori_loop(0, 2, self_near, 0)
+    self_chunk(1)
     forward(1)
     plane_out(2)
+    self_chunk(3)
     forwarded(1)
     cross(1, 0)
     z_in((4, 5, 8), (2,))
@@ -469,17 +466,17 @@
     to_core(0)
     cross(1, 1)
     to_plane(0)
+    forward(2)
+    plane_out(3)
     chunks(1, (2, lambda i: 3 - i))
     to_core(1)
     self_chunk(2)
-    forward(2)
-    plane_out(3)
     forwarded(2)
     cross(2, 0)
     to_plane(1)
+    forward(3)
     chunks(2, (3, lambda i: i + 1))
     to_core(2)
-    forward(3)
     for c in own_p:
         c.wait()
     z_in((6, 7, 9), (1, 3, 2))
@@ -504,6 +501,9 @@
         return 0
 
     lax.fori_loop(0, 3, last_part, 0)
+    moved_s.wait_recv()
+    fin_s[...] = ((acc_s[:, K] + ss_r[...].astype(f32)) * scaled).astype(bf16)
+    spread(2, fin_s, dk_o, dv_o)
     cross(3, 0)
     to_core(3)
     finish_dq(0)
@@ -511,9 +511,6 @@
     moved_l.wait_recv()
     final(0)
     to_plane(3)
-    moved_s.wait_recv()
-    fin_s[...] = ((acc_s[:, K] + ss_r[...].astype(f32)) * scaled).astype(bf16)
-    spread(2, fin_s, dk_o, dv_o)
     final(1)
     final(2)
     final(3)

time: 119 us -> 114 us (0.958)
  Pallas kernels: 118 us -> 113 us
    pallas_call x1, Pallas kernels: 115 us -> 110 us  [shards(): pl.pallas_call(body, out_shape=results, in_specs=[smem, smem, hbm, hbm, h...]
where the time goes in v3:
time: 114 us; the launch traced here: 113 us
  Pallas kernels  113 us (99%)
    pallas_call x1, Pallas kernels, shards(): pl.pallas_call(body, out_shape=results, in_specs=[smem, smem, hbm, hbm, h...  110 us
    pallas_call x1, Pallas kernels, shards(): pl.pallas_call(place, out_shape=results, in_specs=[hbm] * 6, out_specs=(h...  2.59 us

profile of v3, /device:TPU:1, one launch (start us, length us, event | category | flops | bytes accessed | tf_op | source)
XLA Modules:
  0.0 113.5 jit_solution(16438757560076497082)
XLA Ops:
  0.6 110.1 %shard_map.190 = (bf16[128,4096]{1,0:T(8,128)(2,1)}, bf16[128,512]{1,0:T(8,128)(2,1)}, bf16[128,512]{1,0:T(8,128)(2,1)}, bf16[64,4096]{1,0:T(8,128)(2,1)}, bf16[...) custom-call(s32[8,16]{1,0:T(8,128)} %bitcast.1, s32[16]{0:T(128)} %lens.1, bf16[128,4096]{1,0:T(8,128)(2,1)} %q.1, ...), custom_call_target="tpu_custom_call" | custom-call | tf_op jit(solution)/shard_map/pallas_call | solution.py:586
  110.7 2.6 %shard_map.191 = (bf16[128,4096]{1,0:T(8,128)(2,1)}, bf16[128,512]{1,0:T(8,128)(2,1)}, bf16[128,512]{1,0:T(8,128)(2,1)}, bf16[64,4096]{1,0:T(8,128)(2,1)}, bf16[...) custom-call(bf16[128,4096]{1,0:T(8,128)(2,1)} %get-tuple-element.12.refs_0_, bf16[128,512]{1,0:T(8,128)(2,1)} %get-tuple-element.13.refs_1_, ...), custom_call_target="tpu_custom_call" | custom-call | tf_op jit(solution)/shard_map/pallas_call | solution.py:600
